TPU v7x, 1024 devices: a whole 4x4x32 slice. The times are simulated.
1024 devices in a mesh: energy: 256 (over z, y, x_lo), slab: 4 (over x_hi, core).
Axes of the slice: x: 4 (x_hi: 2, x_lo: 2; x = x_hi * 2 + x_lo), y: 4, z: 32, core: 2. Of those that a mesh axis runs over, the one named last changes fastest.
Arguments:
- green_free: bfloat16 [256, 4, 2, 256, 256], P('energy', 'slab')
- coupling: bfloat16 [4, 2, 256, 256], P('slab'), may hold values from -0.25 to 0.25
- screened: bfloat16 [8, 4, 2, 256, 256], P(None, 'slab'), may hold values from -6 to 6
- shift_offsets: int32 [8], replicated, may hold values from -1 to 1, as said below
Outputs:
- green: bfloat16 [256, 4, 2, 256, 256], P('energy', 'slab')
- sigma: float32 [256, 4, 2, 256, 256], P('energy', 'slab')
Inputs may be any that keep to these rules, and one draw needn't show every extreme that they name: `shift_offsets`: offsets lie within one device's energy points on either side; both ends, -1 and 1, occur in every draw.
All inputs are finite; a program needn't handle non-finite values.
Results may differ from a plain program's by a relative error of at most 0.0061.
Values may be sent and summed in bfloat16 or wider, within the bound.
A program may use at most 32 MiB of HBM per device.

v0:
```python
import jax
import jax.numpy as jnp
from jax import lax
from jax.sharding import PartitionSpec as P


def from_behind(block, axis, distance):
    devices = range(lax.axis_size(axis))
    route = [(i - distance, i) for i in devices if i - distance in devices]
    return lax.ppermute(block, axis, route)


def with_halo(block, sides, width):
    for axis, dim in sides:
        count = lax.axis_size(axis)
        forward = [(i, i + 1) for i in range(count - 1)]
        forward.append((count - 1, 0))
        backward = [(target, source) for source, target in forward]
        low = lax.ppermute(
            lax.slice_in_dim(block, block.shape[dim] - width, None, axis=dim), axis, forward
        )
        high = lax.ppermute(lax.slice_in_dim(block, 0, width, axis=dim), axis, backward)
        block = jnp.concatenate([low, block, high], axis=dim)
    return block


def complex_product(first, second, form):
    first_re = first[..., 0, :, :]
    first_im = first[..., 1, :, :]
    second_re = second[..., 0, :, :]
    second_im = second[..., 1, :, :]
    real = jnp.einsum(form, first_re, second_re, preferred_element_type=jnp.float32) - jnp.einsum(
        form, first_im, second_im, preferred_element_type=jnp.float32
    )
    imag = jnp.einsum(form, first_re, second_im, preferred_element_type=jnp.float32) + jnp.einsum(
        form, first_im, second_re, preferred_element_type=jnp.float32
    )
    return jnp.stack([real, imag], axis=-3)


def adjoint(block):
    real = jnp.swapaxes(block[..., 0, :, :], -1, -2)
    imag = -jnp.swapaxes(block[..., 1, :, :], -1, -2)
    return jnp.stack([real, imag], axis=-3)


def shards(green_free, coupling, screened, shift_offsets):
    energies = green_free.shape[0]
    slabs = green_free.shape[1]
    orbitals = green_free.shape[3]
    left_map = complex_product(green_free, coupling, "esij,sjk->esik").astype(jnp.bfloat16)
    right_map = complex_product(adjoint(coupling), green_free, "sij,esjk->esik").astype(
        jnp.bfloat16
    )

    def sweep(incoming):
        current = incoming
        middle = complex_product(left_map[:, 0], current, "eij,ejk->eik").astype(jnp.bfloat16)
        current = (
            green_free[:, 0].astype(jnp.float32)
            + complex_product(middle, right_map[:, 0], "eij,ejk->eik")
        ).astype(jnp.bfloat16)
        results = [current]
        return jnp.stack(results, axis=1)

    boundary = jnp.zeros((energies, 2, orbitals, orbitals), jnp.bfloat16)
    incoming = boundary
    for segment_no in range(lax.axis_size("slab") - 1):
        swept = sweep(incoming)
        incoming = from_behind(swept[:, -1], "slab", 1)
    green = sweep(incoming)
    shape_one = (energies, slabs, orbitals, orbitals)
    padded = with_halo(green, (("energy", 0),), energies)
    real_sum = jnp.zeros(shape_one, jnp.float32)
    imag_sum = jnp.zeros(shape_one, jnp.float32)
    for shift_no in range(screened.shape[0]):
        begin = energies - shift_offsets[shift_no]
        moved = lax.dynamic_slice_in_dim(padded, begin, energies, 0).astype(jnp.float32)
        weight = screened[shift_no].astype(jnp.float32)
        moved_re = moved[:, :, 0]
        moved_im = moved[:, :, 1]
        weight_re = weight[None, :, 0]
        weight_im = weight[None, :, 1]
        real_sum = real_sum + moved_re * weight_re - moved_im * weight_im
        imag_sum = imag_sum + moved_re * weight_im + moved_im * weight_re
    sigma = jnp.stack([-imag_sum, real_sum], axis=2)
    return (green, sigma)


def solution(mesh):
    placed = (
        P("energy", "slab", None, None, None),
        P("slab", None, None, None),
        P(None, "slab", None, None, None),
        P(),
    )
    return jax.shard_map(
        shards,
        mesh=mesh,
        in_specs=placed,
        out_specs=(P("energy", "slab", None, None, None), P("energy", "slab", None, None, None)),
        check_vma=False,
    )
```

profile of v0, /device:TPU:1, one launch (start us, length us, event | category | flops | bytes accessed | tf_op | source)
XLA Modules:
  0.0 83.4 jit_solution(3701337554972136951)
XLA Ops:
  0.7 1.2 %fusion.31 = f32[256,256]{1,0:T(8,128)S(1)} fusion(bf16[1,1,2,256,256]{4,3,2,1,0:T(8,128)(2,1)} %param.4, bf16[1,2,256,256]{3,2,1,0:T(8,128)(2,1)} %param.5), kind=kOutput, calls=%fused_computation.95 | convolution fusion | flops 33554432 | bytes 524288 | tf_op jit(solution)/shard_map/sij,esjk->esik/dot_general | solution.py:35
  1.9 1.2 %fusion.40 = f32[256,256]{1,0:T(8,128)S(1)} fusion(bf16[1,1,2,256,256]{4,3,2,1,0:T(8,128)(2,1)} %param.4, bf16[1,2,256,256]{3,2,1,0:T(8,128)(2,1)} %param.5), kind=kOutput, calls=%fused_computation.104 | convolution fusion | flops 33554432 | bytes 524288 | tf_op jit(solution)/shard_map/sij,esjk->esik/dot_general | solution.py:32
  3.1 1.2 %fusion.36 = f32[256,256]{1,0:T(8,128)S(1)} fusion(bf16[1,2,256,256]{3,2,1,0:T(8,128)(2,1)} %param.5, bf16[1,1,2,256,256]{4,3,2,1,0:T(8,128)(2,1)} %param.4), kind=kOutput, calls=%fused_computation.100 | convolution fusion | flops 33554432 | bytes 524288 | tf_op jit(solution)/shard_map/esij,sjk->esik/dot_general | solution.py:35
  4.3 1.2 %fusion.43 = f32[256,256]{1,0:T(8,128)S(1)} fusion(bf16[1,1,2,256,256]{4,3,2,1,0:T(8,128)(2,1)} %param.4, bf16[1,2,256,256]{3,2,1,0:T(8,128)(2,1)} %param.5), kind=kOutput, calls=%fused_computation.107 | convolution fusion | flops 33554432 | bytes 524288 | tf_op jit(solution)/shard_map/esij,sjk->esik/dot_general | solution.py:32
  5.5 0.2 fusion.18
  5.7 0.2 fusion.19
  6.0 0.2 fusion.20
  6.2 0.2 fusion.73
  6.4 0.2 fusion.21
  6.7 0.2 add_convert_fusion
  7.1 0.2 fusion.80
  7.4 0.2 fusion.6
  7.6 0.2 fusion.7
  7.9 6.0 %collective-permute-start = (bf16[1,2,256,256]{3,2,1,0:T(8,128)(2,1)S(1)}, bf16[1,2,256,256]{3,2,1,0:T(8,128)(2,1)S(1)}, u32[]{:S(2)}, u32[]{:S(2)}) collective-permute-start(bf16[1,2,256,256]{3,2,1,0:T(8,128)(2,1)S(1)} %fusion.25), channel_id=1, source_target_pairs={{0,1},{1,2},{2,3},{4,5},{5,6},{6,7},{8,9},{9,10},{10,11},{12,13},{... | collective-permute-start | bytes 786440 | tf_op jit(solution)/shard_map/ppermute | solution.py:10
  14.0 10.4 %collective-permute-done = bf16[1,2,256,256]{3,2,1,0:T(8,128)(2,1)S(1)} collective-permute-done((bf16[1,2,256,256]{3,2,1,0:T(8,128)(2,1)S(1)}, bf16[1,2,256,256]{3,2,1,0:T(8,128)(2,1)S(1)}, u32[]{:S(2)}, u32[]{:S(2)}) %collective-permute-start) | collective-permute-done | bytes 262176 | tf_op jit(solution)/shard_map/ppermute | solution.py:10
  24.4 0.2 fusion.50
  24.6 0.2 fusion.12
  25.1 0.2 fusion.82
  25.3 0.2 fusion.49
  25.5 0.2 fusion.13
  25.7 0.2 fusion.4
  26.0 0.2 fusion.5
  26.3 1.9 %collective-permute-start.1 = (bf16[1,2,256,256]{3,2,1,0:T(8,128)(2,1)S(1)}, bf16[1,2,256,256]{3,2,1,0:T(8,128)(2,1)S(1)}, u32[]{:S(2)}, u32[]{:S(2)}) collective-permute-start(bf16[1,2,256,256]{3,2,1,0:T(8,128)(2,1)S(1)} %fusion.26), channel_id=1, source_target_pairs={{0,1},{1,2},{2,3},{4,5},{5,6},{6,7},{8,9},{9,10},{10,11},{12,13},{... | collective-permute-start | bytes 786440 | tf_op jit(solution)/shard_map/ppermute | solution.py:10
  28.2 3.3 %collective-permute-done.1 = bf16[1,2,256,256]{3,2,1,0:T(8,128)(2,1)S(1)} collective-permute-done((bf16[1,2,256,256]{3,2,1,0:T(8,128)(2,1)S(1)}, bf16[1,2,256,256]{3,2,1,0:T(8,128)(2,1)S(1)}, u32[]{:S(2)}, u32[]{:S(2)}) %collective-permute-start.1) | collective-permute-done | bytes 262176 | tf_op jit(solution)/shard_map/ppermute | solution.py:10
  31.5 0.2 fusion.52
  31.7 0.2 fusion.14
  32.0 0.2 fusion.85
  32.4 0.2 fusion.51
  32.7 0.2 fusion.15
  32.9 0.2 fusion.2
  33.1 0.2 fusion.3
  33.4 5.9 %collective-permute-start.2 = (bf16[1,2,256,256]{3,2,1,0:T(8,128)(2,1)S(1)}, bf16[1,2,256,256]{3,2,1,0:T(8,128)(2,1)S(1)}, u32[]{:S(2)}, u32[]{:S(2)}) collective-permute-start(bf16[1,2,256,256]{3,2,1,0:T(8,128)(2,1)S(1)} %fusion.27), channel_id=1, source_target_pairs={{0,1},{1,2},{2,3},{4,5},{5,6},{6,7},{8,9},{9,10},{10,11},{12,13},{... | collective-permute-start | bytes 786440 | tf_op jit(solution)/shard_map/ppermute | solution.py:10
  39.3 0.7 fusion.79
  49.8 0.2 fusion.54
  50.1 0.2 fusion.16
  50.8 0.2 fusion.53
  51.0 0.2 fusion.17
  51.2 0.2 fusion
  51.4 0.2 fusion.1
  51.8 17.7 %collective-permute-start.4 = (bf16[1,1,2,256,256]{4,3,2,1,0:T(8,128)(2,1)S(1)}, bf16[1,1,2,256,256]{4,3,2,1,0:T(8,128)(2,1)S(1)}, u32[]{:S(2)}, u32[]{:S(2)}) collective-permute-start(bf16[1,1,2,256,256]{4,3,2,1,0:T(8,128)(2,1)S(1)} %fusion.28), channel_id=1, source_target_pairs={{4,0},{8,4},{12,8},{16,12},{20,16},{24,20},{28,24},{32,28},{36,32}... | collective-permute-start | bytes 786440 | tf_op jit(solution)/shard_map/ppermute | solution.py:22
  69.5 1.9 %collective-permute-start.3 = (bf16[1,1,2,256,256]{4,3,2,1,0:T(8,128)(2,1)S(1)}, bf16[1,1,2,256,256]{4,3,2,1,0:T(8,128)(2,1)S(1)}, u32[]{:S(2)}, u32[]{:S(2)}) collective-permute-start(bf16[1,1,2,256,256]{4,3,2,1,0:T(8,128)(2,1)S(1)} %fusion.28), channel_id=1, source_target_pairs={{0,4},{4,8},{8,12},{12,16},{16,20},{20,24},{24,28},{28,32},{32,36}... | collective-permute-start | bytes 786440 | tf_op jit(solution)/shard_map/ppermute | solution.py:19
  71.4 0.4 bitcast_convert_fusion.7
  71.9 0.9 %collective-permute-done.4 = bf16[1,1,2,256,256]{4,3,2,1,0:T(8,128)(2,1)S(1)} collective-permute-done((bf16[1,1,2,256,256]{4,3,2,1,0:T(8,128)(2,1)S(1)}, bf16[1,1,2,256,256]{4,3,2,1,0:T(8,128)(2,1)S(1)}, u32[]{:S(2)}, u32[]{:S(2)}) %collective-permute-start.4) | collective-permute-done | bytes 262176 | tf_op jit(solution)/shard_map/ppermute | solution.py:22
  72.8 8.1 %collective-permute-done.3 = bf16[1,1,2,256,256]{4,3,2,1,0:T(8,128)(2,1)S(1)} collective-permute-done((bf16[1,1,2,256,256]{4,3,2,1,0:T(8,128)(2,1)S(1)}, bf16[1,1,2,256,256]{4,3,2,1,0:T(8,128)(2,1)S(1)}, u32[]{:S(2)}, u32[]{:S(2)}) %collective-permute-start.3) | collective-permute-done | bytes 262176 | tf_op jit(solution)/shard_map/ppermute | solution.py:19
  81.0 0.5 dynamic-slice_convert_fusion
  81.5 0.5 negate_bitcast_fusion
  82.0 0.5 subtract_bitcast_fusion
  82.6 0.8 pad_maximum_fusion.1
  (21 shorter events, 1.5 us)
Async XLA Ops:
  0.6 4.9 %copy-start = (bf16[1,1,2,256,256]{4,3,2,1,0:T(8,128)(2,1)S(1)}, bf16[1,1,2,256,256]{4,3,2,1,0:T(8,128)(2,1)}, u32[]{:S(2)}) copy-start(bf16[1,1,2,256,256]{4,3,2,1,0:T(8,128)(2,1)} %param.4) | copy-start | bytes 786436
  0.6 4.9 %copy-start.1 = (bf16[1,2,256,256]{3,2,1,0:T(8,128)(2,1)S(1)}, bf16[1,2,256,256]{3,2,1,0:T(8,128)(2,1)}, u32[]{:S(2)}) copy-start(bf16[1,2,256,256]{3,2,1,0:T(8,128)(2,1)} %param.5) | copy-start | bytes 786436
  7.9 16.5 %collective-permute-start = (bf16[1,2,256,256]{3,2,1,0:T(8,128)(2,1)S(1)}, bf16[1,2,256,256]{3,2,1,0:T(8,128)(2,1)S(1)}, u32[]{:S(2)}, u32[]{:S(2)}) collective-permute-start(bf16[1,2,256,256]{3,2,1,0:T(8,128)(2,1)S(1)} %fusion.25), channel_id=1, source_target_pairs={{0,1},{1,2},{2,3},{4,5},{5,6},{6,7},{8,9},{9,10},{10,11},{12,13},{... | collective-permute-start | bytes 786440 | tf_op jit(solution)/shard_map/ppermute | solution.py:10
  26.3 5.2 %collective-permute-start.1 = (bf16[1,2,256,256]{3,2,1,0:T(8,128)(2,1)S(1)}, bf16[1,2,256,256]{3,2,1,0:T(8,128)(2,1)S(1)}, u32[]{:S(2)}, u32[]{:S(2)}) collective-permute-start(bf16[1,2,256,256]{3,2,1,0:T(8,128)(2,1)S(1)} %fusion.26), channel_id=1, source_target_pairs={{0,1},{1,2},{2,3},{4,5},{5,6},{6,7},{8,9},{9,10},{10,11},{12,13},{... | collective-permute-start | bytes 786440 | tf_op jit(solution)/shard_map/ppermute | solution.py:10
  32.2 7.1 %copy-start.4 = (s32[8]{0:T(128)S(1)}, s32[8]{0:T(128)}, u32[]{:S(2)}) copy-start(s32[8]{0:T(128)} %param.7) | copy-start | bytes 100
  33.4 16.4 %collective-permute-start.2 = (bf16[1,2,256,256]{3,2,1,0:T(8,128)(2,1)S(1)}, bf16[1,2,256,256]{3,2,1,0:T(8,128)(2,1)S(1)}, u32[]{:S(2)}, u32[]{:S(2)}) collective-permute-start(bf16[1,2,256,256]{3,2,1,0:T(8,128)(2,1)S(1)} %fusion.27), channel_id=1, source_target_pairs={{0,1},{1,2},{2,3},{4,5},{5,6},{6,7},{8,9},{9,10},{10,11},{12,13},{... | collective-permute-start | bytes 786440 | tf_op jit(solution)/shard_map/ppermute | solution.py:10
  50.5 20.9 %copy-start.2 = (bf16[8,1,2,256,256]{4,3,2,1,0:T(8,128)(2,1)S(1)}, bf16[8,1,2,256,256]{4,3,2,1,0:T(8,128)(2,1)}, u32[]{:S(2)}) copy-start(bf16[8,1,2,256,256]{4,3,2,1,0:T(8,128)(2,1)} %param.6) | copy-start | bytes 6291460
  51.7 29.2 %copy-start.3 = (bf16[1,1,2,256,256]{4,3,2,1,0:T(8,128)(2,1)}, bf16[1,1,2,256,256]{4,3,2,1,0:T(8,128)(2,1)S(1)}, u32[]{:S(2)}) copy-start(bf16[1,1,2,256,256]{4,3,2,1,0:T(8,128)(2,1)S(1)} %fusion.28) | copy-start | bytes 786436
  51.8 21.0 %collective-permute-start.4 = (bf16[1,1,2,256,256]{4,3,2,1,0:T(8,128)(2,1)S(1)}, bf16[1,1,2,256,256]{4,3,2,1,0:T(8,128)(2,1)S(1)}, u32[]{:S(2)}, u32[]{:S(2)}) collective-permute-start(bf16[1,1,2,256,256]{4,3,2,1,0:T(8,128)(2,1)S(1)} %fusion.28), channel_id=1, source_target_pairs={{4,0},{8,4},{12,8},{16,12},{20,16},{24,20},{28,24},{32,28},{36,32}... | collective-permute-start | bytes 786440 | tf_op jit(solution)/shard_map/ppermute | solution.py:22
  69.5 11.4 %collective-permute-start.3 = (bf16[1,1,2,256,256]{4,3,2,1,0:T(8,128)(2,1)S(1)}, bf16[1,1,2,256,256]{4,3,2,1,0:T(8,128)(2,1)S(1)}, u32[]{:S(2)}, u32[]{:S(2)}) collective-permute-start(bf16[1,1,2,256,256]{4,3,2,1,0:T(8,128)(2,1)S(1)} %fusion.28), channel_id=1, source_target_pairs={{0,4},{4,8},{8,12},{12,16},{16,20},{20,24},{24,28},{28,32},{32,36}... | collective-permute-start | bytes 786440 | tf_op jit(solution)/shard_map/ppermute | solution.py:19
where the time goes:
time: 83.8 us; the launch traced here: 83.4 us
  starting transfers between devices  33.5 us (40%)
  waiting for transfers between devices  22.7 us (27%)
  matrix products  12.4 us (15%)
  between operations  10.9 us (13%)
  other arithmetic  3.2 us (4%)
    ppermute x1, starting transfers between devices, with_halo(): lax.ppermute(lax.slice_in_dim(block, 0, width, axis=dim), axis, backward)  17.7 us
    ppermute x3, starting transfers between devices, from_behind(): return lax.ppermute(block, axis, route)  13.8 us
    ppermute x3, waiting for transfers between devices, from_behind(): return lax.ppermute(block, axis, route)  13.7 us
    ppermute x1, waiting for transfers between devices, with_halo(): lax.ppermute(lax.slice_in_dim(block, block.shape[dim] - width, None, axis...  8.13 us
    dot_general x10, matrix products, complex_product(): jnp.einsum(form, first_re, second_re, preferred_element_type=jnp.float32)  4.16 us
    dot_general x9, matrix products, complex_product(): jnp.einsum(form, first_re, second_im, preferred_element_type=jnp.float32)  3.98 us
    dot_general x10, matrix products, complex_product(): jnp.einsum(form, first_im, second_im, preferred_element_type=jnp.float32)  2.22 us
    dot_general x9, matrix products, complex_product(): jnp.einsum(form, first_im, second_re, preferred_element_type=jnp.float32)  2.02 us
  transfers between devices with their start and end apart: 5, of which 4 were waited for; matrix products, arithmetic and copies ran while one was open for 1% of the time, Pallas kernels for 0%

commit v1 on v0

v1 whole, which is shorter than its diff:
```python
import functools

import jax
import jax.numpy as jnp
from jax import lax
from jax.experimental import pallas as pl
from jax.experimental.pallas import tpu as pltpu
from jax.sharding import PartitionSpec as P

MESH = pl.DeviceIdType.MESH
CHUNKS = 4


def dot(a, b):
    return jnp.dot(a, b, preferred_element_type=jnp.float32)


def dot_t(a, b):
    return lax.dot_general(a, b, (((0,), (0,)), ((), ())), preferred_element_type=jnp.float32)


def complex_dot(first, second_re, second_im):
    half = first.shape[0] // 2
    by_re = dot(first, second_re)
    by_im = dot(first, second_im)
    return by_re[:half] - by_im[half:], by_im[:half] + by_re[half:]


def kernel(
    energies,
    slabs,
    shift_ref,
    free_hbm,
    coup_hbm,
    scr_hbm,
    green,
    sig,
    free,
    coup,
    scr,
    left,
    right,
    prev,
    near,
    far,
    weight,
    load_sem,
    chain_send,
    chain_recv,
    near_send,
    near_recv,
    far_send,
    far_recv,
):
    e = lax.axis_index("energy")
    s = lax.axis_index("slab")
    shifts = scr.shape[0]
    orb = free.shape[1]
    rows = orb // CHUNKS
    parity = lax.rem(e, 2)
    partner = e + 1 - 2 * parity
    onward = lax.rem(e + 2 - 4 * parity + energies, energies)
    behind = lax.rem(e - 2 + 4 * parity + energies, energies)

    load_free = pltpu.make_async_copy(free_hbm.at[0, 0], free, load_sem.at[0])
    load_coup = pltpu.make_async_copy(coup_hbm.at[0], coup, load_sem.at[1])
    load_free.start()
    load_coup.start()
    loads = []
    for k in range(shifts):
        load = pltpu.make_async_copy(scr_hbm.at[k, 0], scr.at[k], load_sem.at[2 + k])
        load.start()
        loads.append(load)

    barrier = pltpu.get_barrier_semaphore()
    pl.semaphore_signal(barrier, inc=1, device_id=(partner, s), device_id_type=MESH)
    pl.semaphore_signal(barrier, inc=1, device_id=(behind, s), device_id_type=MESH)

    @pl.when(s > 0)
    def _():
        pl.semaphore_signal(barrier, inc=1, device_id=(e, s - 1), device_id_type=MESH)

    chain = pltpu.make_async_remote_copy(
        src_ref=green,
        dst_ref=prev,
        send_sem=chain_send,
        recv_sem=chain_recv,
        device_id=(e, lax.rem(s + 1, slabs)),
        device_id_type=MESH,
    )

    def to_partner(c):
        part = pl.ds(c * rows, rows)
        return pltpu.make_async_remote_copy(
            src_ref=green.at[:, part],
            dst_ref=near.at[:, part],
            send_sem=near_send.at[c],
            recv_sem=near_recv.at[c],
            device_id=(partner, s),
            device_id_type=MESH,
        )

    def to_onward(c):
        part = pl.ds(c * rows, rows)
        return pltpu.make_async_remote_copy(
            src_ref=near.at[:, part],
            dst_ref=far.at[:, part],
            send_sem=far_send.at[c],
            recv_sem=far_recv.at[c],
            device_id=(onward, s),
            device_id_type=MESH,
        )

    def sum_weights():
        for load in loads:
            load.wait()
        near_shift = 2 * parity - 1

        @pl.loop(0, orb // 16)
        def _(step):
            part = pl.ds(pl.multiple_of(step * 16, 16), 16)
            at = [jnp.zeros((2, 16, orb), jnp.float32) for _ in range(3)]
            for k in range(shifts):
                block = scr[k, :, part, :].astype(jnp.float32)
                for slot, value in enumerate((0, near_shift, -near_shift)):
                    at[slot] = at[slot] + jnp.where(shift_ref[k] == value, block, 0.0)
            for slot in range(3):
                weight[slot, :, part, :] = at[slot]

    load_free.wait()

    @pl.when(s == 0)
    def _():
        green[...] = free[...]
        load_coup.wait()

    @pl.when(s > 0)
    def _():
        load_coup.wait()
        stacked = free[...].reshape(2 * orb, orb)
        re, im = complex_dot(stacked, coup[0], coup[1])
        left[0] = re.astype(jnp.bfloat16)
        left[1] = im.astype(jnp.bfloat16)
        rr = dot_t(coup[0], free[0]) + dot_t(coup[1], free[1])
        ri = dot_t(coup[0], free[1]) - dot_t(coup[1], free[0])
        right[0] = rr.astype(jnp.bfloat16)
        right[1] = ri.astype(jnp.bfloat16)

    @pl.when(s >= 2)
    def _():
        sum_weights()

    @pl.when(s < slabs - 1)
    def _():
        pl.semaphore_wait(barrier, 3)

    @pl.when(s == slabs - 1)
    def _():
        pl.semaphore_wait(barrier, 2)

    @pl.when(s > 0)
    def _():
        chain.wait_recv()
        re, im = complex_dot(left[...].reshape(2 * orb, orb), prev[0], prev[1])
        middle = jnp.concatenate([re.astype(jnp.bfloat16), im.astype(jnp.bfloat16)], axis=0)
        re, im = complex_dot(middle, right[0], right[1])
        green[0] = (free[0].astype(jnp.float32) + re).astype(jnp.bfloat16)
        green[1] = (free[1].astype(jnp.float32) + im).astype(jnp.bfloat16)

    @pl.when(s < slabs - 1)
    def _():
        chain.start()

    for c in range(CHUNKS):
        to_partner(c).start()

    @pl.when(s < 2)
    def _():
        sum_weights()

    def term(block, slot, part):
        re = block[0, part, :].astype(jnp.float32)
        im = block[1, part, :].astype(jnp.float32)
        wr = weight[slot, 0, part, :]
        wi = weight[slot, 1, part, :]
        return re * wr - im * wi, re * wi + im * wr

    for c in range(CHUNKS):
        part = pl.ds(c * rows, rows)
        to_partner(c).wait_recv()
        to_onward(c).start()
        own = term(green, 0, part)
        beside = term(near, 1, part)
        sig[0, part, :] = -(own[1] + beside[1])
        sig[1, part, :] = own[0] + beside[0]

    for c in range(CHUNKS):
        part = pl.ds(c * rows, rows)
        to_onward(c).wait_recv()
        beyond = term(far, 2, part)
        sig[0, part, :] = sig[0, part, :] - beyond[1]
        sig[1, part, :] = sig[1, part, :] + beyond[0]

    @pl.when(s < slabs - 1)
    def _():
        chain.wait_send()

    for c in range(CHUNKS):
        to_partner(c).wait_send()
        to_onward(c).wait_send()


def shards(energies, slabs, green_free, coupling, screened, shift_offsets):
    orb = green_free.shape[-1]
    shifts = screened.shape[0]
    block = (2, orb, orb)
    hbm = pl.BlockSpec(memory_space=pltpu.HBM)
    vmem = pl.BlockSpec(memory_space=pltpu.VMEM)
    dma = pltpu.SemaphoreType.DMA
    green, sigma = pl.pallas_call(
        functools.partial(kernel, energies, slabs),
        out_shape=(
            jax.ShapeDtypeStruct(block, jnp.bfloat16),
            jax.ShapeDtypeStruct(block, jnp.float32),
        ),
        in_specs=[pl.BlockSpec(memory_space=pltpu.SMEM), hbm, hbm, hbm],
        out_specs=(vmem, vmem),
        scratch_shapes=[
            pltpu.VMEM(block, jnp.bfloat16),
            pltpu.VMEM(block, jnp.bfloat16),
            pltpu.VMEM((shifts, *block), jnp.bfloat16),
            pltpu.VMEM(block, jnp.bfloat16),
            pltpu.VMEM(block, jnp.bfloat16),
            pltpu.VMEM(block, jnp.bfloat16),
            pltpu.VMEM(block, jnp.bfloat16),
            pltpu.VMEM(block, jnp.bfloat16),
            pltpu.VMEM((3, *block), jnp.float32),
            dma((2 + shifts,)),
            dma,
            dma,
            dma((CHUNKS,)),
            dma((CHUNKS,)),
            dma((CHUNKS,)),
            dma((CHUNKS,)),
        ],
        compiler_params=pltpu.CompilerParams(
            collective_id=0, has_side_effects=True, vmem_limit_bytes=57 * 2**20
        ),
    )(shift_offsets, green_free, coupling, screened)
    return green.reshape(green_free.shape), sigma.reshape(green_free.shape)


def solution(mesh):
    placed = (
        P("energy", "slab", None, None, None),
        P("slab", None, None, None),
        P(None, "slab", None, None, None),
        P(),
    )
    return jax.shard_map(
        functools.partial(shards, mesh.shape["energy"], mesh.shape["slab"]),
        mesh=mesh,
        in_specs=placed,
        out_specs=(P("energy", "slab", None, None, None), P("energy", "slab", None, None, None)),
        check_vma=False,
    )
```

time: 83.8 us -> 47.5 us (0.57)
  the two profiles are of different devices: /device:TPU:1 before, /device:TPU:5 now
where the time goes in v1:
time: 47.5 us; the launch traced here: 47.2 us
  Pallas kernels  43.1 us (91%)
  local copies, waits for them, and re-layouts  3.54 us (7%)
  between operations  0.64 us (1%)
    pallas_call x1, Pallas kernels, shards(): pl.pallas_call(functools.partial(kernel, energies, slabs), out_shape=(jax...  43.1 us
    unnamed x2, local copies, waits for them, and re-layouts  3.54 us

profile of v1, /device:TPU:5, one launch (start us, length us, event | category | flops | bytes accessed | tf_op | source)
XLA Modules:
  0.0 47.2 jit_solution(646257696374303961)
XLA Ops:
  0.6 43.1 %shard_map.59 = (bf16[2,256,256]{2,1,0:T(8,128)(2,1)}, f32[2,256,256]{2,1,0:T(8,128)}) custom-call(s32[8]{0:T(128)} %shift_ref.1, bf16[1,1,2,256,256]{4,3,2,1,0:T(8,128)(2,1)} %free_hbm.1, bf16[1,2,256,256]{3,2,1,0:T(8,128)(2,1)} %coup_hbm.1, bf16[8,1,2,256,256]{4,3,2,1,0:T(8,128)(2,1)} %scr_hbm.1), custom_call_target="tpu_custom_call" | custom-call | tf_op jit(solution)/shard_map/pallas_call | solution.py:220
  43.7 1.7 %copy.8 = bf16[1,1,2,256,256]{4,3,2,1,0:T(8,128)(2,1)} copy(bf16[1,1,2,256,256]{4,3,2,1,0:T(8,128)(2,1)} %bitcast.3) | data formatting | bytes 524288
  45.4 1.9 %copy.9 = f32[1,1,2,256,256]{4,3,2,1,0:T(8,128)} copy(f32[1,1,2,256,256]{4,3,2,1,0:T(8,128)} %bitcast.2) | data formatting | bytes 1048576

commit v2 on v1

v2 whole, which is shorter than its diff:
```python
import functools

import jax
import jax.numpy as jnp
from jax import lax
from jax.experimental import pallas as pl
from jax.experimental.pallas import tpu as pltpu
from jax.sharding import PartitionSpec as P

MESH = pl.DeviceIdType.MESH
CHUNKS = 4
STEPS = 2
CHAIN, CROSS, BEYOND, NEAR, FAR, FREE_NEAR, FREE_FAR = range(7)
OWN, BESIDE, REMOTE = range(3)


def dot(a, b):
    return jnp.dot(a, b, preferred_element_type=jnp.float32)


def dot_t(a, b):
    return lax.dot_general(a, b, (((0,), (0,)), ((), ())), preferred_element_type=jnp.float32)


def complex_dot(first, second_re, second_im):
    half = first.shape[0] // 2
    by_re = dot(first, second_re)
    by_im = dot(first, second_im)
    return by_re[:half] - by_im[half:], by_im[:half] + by_re[half:]


def kernel(
    energies,
    shift_ref,
    free_hbm,
    coup_hbm,
    scr_hbm,
    green,
    sig,
    free,
    coup,
    scr,
    left,
    right,
    middle,
    chain_in,
    cross_in,
    beyond_in,
    near,
    far,
    free_near,
    free_far,
    weight,
    load_sem,
    send_sem,
    recv_sem,
):
    e = lax.axis_index("energy")
    s = lax.axis_index("slab")
    shifts = scr.shape[0]
    orb = free.shape[1]
    rows = orb // CHUNKS
    parity = lax.rem(e, 2)
    partner = e + 1 - 2 * parity
    onward = lax.rem(e + 2 - 4 * parity + energies, energies)
    behind = lax.rem(e - 2 + 4 * parity + energies, energies)
    landing = (chain_in, cross_in, beyond_in, near, far, free_near, free_far)

    load_free = pltpu.make_async_copy(free_hbm.at[0, 0], free, load_sem.at[0])
    load_coup = pltpu.make_async_copy(coup_hbm.at[0], coup, load_sem.at[1])
    loads = [
        pltpu.make_async_copy(scr_hbm.at[k, 0], scr.at[k], load_sem.at[2 + k])
        for k in range(shifts)
    ]
    barrier = pltpu.get_barrier_semaphore()

    def greet(device):
        pl.semaphore_signal(barrier, inc=1, device_id=device, device_id_type=MESH)

    greet((partner, s))
    greet((behind, s))

    @pl.when(s == 1)
    def _():
        greet((e, 0))

    @pl.when(s == 2)
    def _():
        greet((partner, 1))

    @pl.when(s == 3)
    def _():
        greet((e, 2))

    load_free.start()
    load_coup.start()
    for load in loads:
        load.start()

    def move(kind, source, device, c):
        part = pl.ds(c * rows, rows)
        return pltpu.make_async_remote_copy(
            src_ref=source.at[:, part],
            dst_ref=landing[kind].at[:, part],
            send_sem=send_sem.at[kind, c],
            recv_sem=recv_sem.at[kind, c],
            device_id=device,
            device_id_type=MESH,
        )

    def arrived(kind, c):
        move(kind, free, (partner, s), c).wait_recv()

    def all_arrived(kind):
        for c in range(CHUNKS):
            arrived(kind, c)

    def sent(kind):
        for c in range(CHUNKS):
            move(kind, free, (partner, s), c).wait_send()

    def maps(block, slot):
        re, im = complex_dot(block[...].reshape(2 * orb, orb), coup[0], coup[1])
        left[slot, 0] = re.astype(jnp.bfloat16)
        left[slot, 1] = im.astype(jnp.bfloat16)
        re = dot_t(coup[0], block[0]) + dot_t(coup[1], block[1])
        im = dot_t(coup[0], block[1]) - dot_t(coup[1], block[0])
        right[slot, 0] = re.astype(jnp.bfloat16)
        right[slot, 1] = im.astype(jnp.bfloat16)

    def advance(slot, before, block, result, done=None):
        re, im = complex_dot(left[slot].reshape(2 * orb, orb), before[0], before[1])
        middle[0] = re.astype(jnp.bfloat16)
        middle[1] = im.astype(jnp.bfloat16)
        high = orb // STEPS
        for step in range(STEPS):
            part = pl.ds(step * high, high)
            stacked = middle[:, part, :].reshape(2 * high, orb)
            re, im = complex_dot(stacked, right[slot, 0], right[slot, 1])
            result[0, part, :] = (block[0, part, :].astype(jnp.float32) + re).astype(jnp.bfloat16)
            result[1, part, :] = (block[1, part, :].astype(jnp.float32) + im).astype(jnp.bfloat16)
            if done is not None:
                for c in range(step * CHUNKS // STEPS, (step + 1) * CHUNKS // STEPS):
                    done(c)

    def sum_weights():
        for load in loads:
            load.wait()
        near_shift = 2 * parity - 1

        @pl.loop(0, orb // 16)
        def _(step):
            part = pl.ds(pl.multiple_of(step * 16, 16), 16)
            total = [jnp.zeros((2, 16, orb), jnp.float32) for _ in range(3)]
            for k in range(shifts):
                block = scr[k, :, part, :].astype(jnp.float32)
                for slot, value in enumerate((0, near_shift, -near_shift)):
                    total[slot] = total[slot] + jnp.where(shift_ref[k] == value, block, 0.0)
            for slot in range(3):
                weight[slot, :, part, :] = total[slot]

    def term(block, slot, part):
        re = block[0, part, :].astype(jnp.float32)
        im = block[1, part, :].astype(jnp.float32)
        weight_re = weight[slot, 0, part, :]
        weight_im = weight[slot, 1, part, :]
        return re * weight_re - im * weight_im, re * weight_im + im * weight_re

    def begin_sigma(c):
        part = pl.ds(c * rows, rows)
        own = term(green, OWN, part)
        beside = term(near, BESIDE, part)
        sig[0, part, :] = -(own[1] + beside[1])
        sig[1, part, :] = own[0] + beside[0]

    def end_sigma(c):
        part = pl.ds(c * rows, rows)
        remote = term(far, REMOTE, part)
        sig[0, part, :] = sig[0, part, :] - remote[1]
        sig[1, part, :] = sig[1, part, :] + remote[0]

    @pl.when(s == 0)
    def _():
        load_free.wait()
        pl.semaphore_wait(barrier, 3)
        for c in range(CHUNKS):
            move(CHAIN, free, (e, 1), c).start()
        for c in range(CHUNKS):
            move(NEAR, free, (partner, s), c).start()
        green[...] = free[...]
        sum_weights()
        for c in range(CHUNKS):
            arrived(NEAR, c)
            move(FAR, near, (onward, s), c).start()
            begin_sigma(c)
        for c in range(CHUNKS):
            arrived(FAR, c)
            end_sigma(c)
        load_coup.wait()
        sent(CHAIN)
        sent(NEAR)
        sent(FAR)

    @pl.when(s == 1)
    def _():
        load_free.wait()
        load_coup.wait()
        maps(free, OWN)
        pl.semaphore_wait(barrier, 3)
        all_arrived(CHAIN)
        advance(OWN, chain_in, free, green, lambda c: move(CROSS, green, (partner, 2), c).start())
        for c in range(CHUNKS):
            move(NEAR, green, (partner, s), c).start()
        sum_weights()
        for c in range(CHUNKS):
            arrived(NEAR, c)
            move(CHAIN, near, (partner, 2), c).start()
            move(FAR, near, (onward, s), c).start()
            begin_sigma(c)
        for c in range(CHUNKS):
            arrived(FAR, c)
            end_sigma(c)
        sent(CROSS)
        sent(NEAR)
        sent(CHAIN)
        sent(FAR)

    @pl.when(s == 2)
    def _():
        load_free.wait()
        pl.semaphore_wait(barrier, 3)
        for c in range(CHUNKS):
            move(FREE_NEAR, free, (partner, s), c).start()
        load_coup.wait()
        maps(free, OWN)
        sum_weights()
        all_arrived(FREE_NEAR)
        maps(free_near, BESIDE)
        all_arrived(CROSS)

        def hand_on(c):
            move(FAR, near, (onward, s), c).start()
            move(CROSS, near, (e, 3), c).start()

        advance(BESIDE, cross_in, free_near, near, hand_on)
        all_arrived(CHAIN)
        advance(OWN, chain_in, free, green, lambda c: move(CHAIN, green, (e, 3), c).start())
        for c in range(CHUNKS):
            arrived(FAR, c)
            move(BEYOND, far, (e, 3), c).start()
            begin_sigma(c)
            end_sigma(c)
        sent(FREE_NEAR)
        sent(FAR)
        sent(CROSS)
        sent(CHAIN)
        sent(BEYOND)

    @pl.when(s == 3)
    def _():
        load_free.wait()
        load_coup.wait()
        maps(free, OWN)
        sum_weights()
        pl.semaphore_wait(barrier, 2)
        for c in range(CHUNKS):
            move(FREE_NEAR, free, (partner, s), c).start()
        for c in range(CHUNKS):
            arrived(FREE_NEAR, c)
            move(FREE_FAR, free_near, (onward, s), c).start()
        maps(free_near, BESIDE)
        all_arrived(CROSS)
        advance(BESIDE, cross_in, free_near, near)
        all_arrived(FREE_FAR)
        maps(free_far, REMOTE)
        all_arrived(CHAIN)
        advance(OWN, chain_in, free, green)
        for c in range(CHUNKS):
            begin_sigma(c)
        all_arrived(BEYOND)
        advance(REMOTE, beyond_in, free_far, far, end_sigma)
        sent(FREE_NEAR)
        sent(FREE_FAR)


def store(green, sig, green_hbm, sigma_hbm, sem):
    copies = [
        pltpu.make_async_copy(green, green_hbm.at[0, 0], sem.at[0]),
        pltpu.make_async_copy(sig.at[0], sigma_hbm.at[0, 0, 0], sem.at[1]),
        pltpu.make_async_copy(sig.at[1], sigma_hbm.at[0, 0, 1], sem.at[2]),
    ]
    for copy in copies:
        copy.start()
    for copy in copies:
        copy.wait()


def shards(energies, green_free, coupling, screened, shift_offsets):
    orb = green_free.shape[-1]
    shifts = screened.shape[0]
    block = (2, orb, orb)
    hbm = pl.BlockSpec(memory_space=pltpu.HBM)
    vmem = pl.BlockSpec(memory_space=pltpu.VMEM)
    dma = pltpu.SemaphoreType.DMA
    half = jnp.bfloat16
    green, sigma = pl.pallas_call(
        functools.partial(kernel, energies),
        out_shape=(pltpu.VMEM(block, half), pltpu.VMEM(block, jnp.float32)),
        in_specs=[pl.BlockSpec(memory_space=pltpu.SMEM), hbm, hbm, hbm],
        out_specs=(vmem, vmem),
        scratch_shapes=[
            pltpu.VMEM(block, half),
            pltpu.VMEM(block, half),
            pltpu.VMEM((shifts, *block), half),
            pltpu.VMEM((3, *block), half),
            pltpu.VMEM((3, *block), half),
            *[pltpu.VMEM(block, half)] * 8,
            pltpu.VMEM((3, *block), jnp.float32),
            dma((2 + shifts,)),
            dma((7, CHUNKS)),
            dma((7, CHUNKS)),
        ],
        compiler_params=pltpu.CompilerParams(
            collective_id=0, has_side_effects=True, vmem_limit_bytes=57 * 2**20
        ),
    )(shift_offsets, green_free, coupling, screened)
    return pl.pallas_call(
        store,
        out_shape=(
            jax.ShapeDtypeStruct(green_free.shape, half),
            jax.ShapeDtypeStruct(green_free.shape, jnp.float32),
        ),
        in_specs=[vmem, vmem],
        out_specs=(hbm, hbm),
        scratch_shapes=[dma((3,))],
        compiler_params=pltpu.CompilerParams(vmem_limit_bytes=8 * 2**20),
    )(green, sigma)


def solution(mesh):
    placed = (
        P("energy", "slab", None, None, None),
        P("slab", None, None, None),
        P(None, "slab", None, None, None),
        P(),
    )
    return jax.shard_map(
        functools.partial(shards, mesh.shape["energy"]),
        mesh=mesh,
        in_specs=placed,
        out_specs=(P("energy", "slab", None, None, None), P("energy", "slab", None, None, None)),
        check_vma=False,
    )
```

time: 47.5 us -> 39 us (0.82)
  Pallas kernels: 43.1 us -> 38.1 us
  local copies, waits for them, and re-layouts: 3.54 us -> 0 us
    pallas_call x1 -> x2, Pallas kernels: 43.1 us -> 38.1 us  [the longest x1 37.2 us: shards(): pl.pallas_call(functools.partial(kernel, energies), out_shape=(pltpu.VMEM...]
    unnamed x2 -> x0, local copies, waits for them, and re-layouts: 3.54 us -> none
where the time goes in v2:
time: 39 us; the launch traced here: 38.8 us
  Pallas kernels  38.1 us (98%)
  between operations  0.64 us (2%)
    pallas_call x1, Pallas kernels, shards(): pl.pallas_call(functools.partial(kernel, energies), out_shape=(pltpu.VMEM...  37.2 us
    pallas_call x1, Pallas kernels, shards(): pl.pallas_call(store, out_shape=(jax.ShapeDtypeStruct(green_free.shape, h...  0.9 us

profile of v2, /device:TPU:5, one launch (start us, length us, event | category | flops | bytes accessed | tf_op | source)
XLA Modules:
  0.0 38.8 jit_solution(13627168064928909262)
XLA Ops:
  0.6 37.2 %shard_map.59 = (bf16[2,256,256]{2,1,0:T(8,128)(2,1)S(1)}, f32[2,256,256]{2,1,0:T(8,128)S(1)}) custom-call(s32[8]{0:T(128)} %shift_ref.1, bf16[1,1,2,256,256]{4,3,2,1,0:T(8,128)(2,1)} %free_hbm.1, bf16[1,2,256,256]{3,2,1,0:T(8,128)(2,1)} %coup_hbm.1, bf16[8,1,2,256,256]{4,3,2,1,0:T(8,128)(2,1)} %scr_hbm.1), custom_call_target="tpu_custom_call" | custom-call | tf_op jit(solution)/shard_map/pallas_call | solution.py:306
  37.9 0.9 %shard_map.60 = (bf16[1,1,2,256,256]{4,3,2,1,0:T(8,128)(2,1)}, f32[1,1,2,256,256]{4,3,2,1,0:T(8,128)}) custom-call(bf16[2,256,256]{2,1,0:T(8,128)(2,1)S(1)} %get-tuple-element.4.green, f32[2,256,256]{2,1,0:T(8,128)S(1)} %get-tuple-element.5.sig), custom_call_target="tpu_custom_call" | custom-call | tf_op jit(solution)/shard_map/pallas_call | solution.py:327

commit v3 on v2

--- a/solution.py
+++ b/solution.py
@@ -54,6 +54,7 @@
     load_sem,
     send_sem,
     recv_sem,
+    ready,
 ):
     e = lax.axis_index("energy")
     s = lax.axis_index("slab")
@@ -78,7 +79,6 @@
         pl.semaphore_signal(barrier, inc=1, device_id=device, device_id_type=MESH)
 
     greet((partner, s))
-    greet((behind, s))
 
     @pl.when(s == 1)
     def _():
@@ -87,15 +87,49 @@
     @pl.when(s == 2)
     def _():
         greet((partner, 1))
+        greet((e, 3))
 
     @pl.when(s == 3)
     def _():
         greet((e, 2))
+
+    far_side = jnp.where(s == 2, 3, s)
+
+    @pl.when(onward > e)
+    def _():
+        greet((onward, far_side))
+
+    @pl.when(jnp.logical_and(behind > e, s != 2))
+    def _():
+        greet((behind, s))
+
+    @pl.when(jnp.logical_and(behind > e, s == 3))
+    def _():
+        greet((behind, 2))
 
     load_free.start()
     load_coup.start()
-    for load in loads:
-        load.start()
+
+    def meet(row, senders):
+        below = jnp.where(onward < e, 1, 0) + jnp.where(behind < e, senders, 0)
+        pl.semaphore_wait(barrier, row + below)
+        if senders:
+
+            @pl.when(behind < e)
+            def _():
+                for sender in range(senders):
+                    pl.semaphore_signal(
+                        ready, inc=1, device_id=(behind, s - sender), device_id_type=MESH
+                    )
+
+    def meet_onward():
+        @pl.when(onward > e)
+        def _():
+            pl.semaphore_wait(ready, 1)
+
+    def load_screened():
+        for load in loads:
+            load.start()
 
     def move(kind, source, device, c):
         part = pl.ds(c * rows, rows)
@@ -182,13 +216,15 @@
     @pl.when(s == 0)
     def _():
         load_free.wait()
-        pl.semaphore_wait(barrier, 3)
+        meet(2, 1)
         for c in range(CHUNKS):
             move(CHAIN, free, (e, 1), c).start()
         for c in range(CHUNKS):
             move(NEAR, free, (partner, s), c).start()
+        load_screened()
         green[...] = free[...]
         sum_weights()
+        meet_onward()
         for c in range(CHUNKS):
             arrived(NEAR, c)
             move(FAR, near, (onward, s), c).start()
@@ -206,12 +242,14 @@
         load_free.wait()
         load_coup.wait()
         maps(free, OWN)
-        pl.semaphore_wait(barrier, 3)
+        meet(2, 1)
         all_arrived(CHAIN)
         advance(OWN, chain_in, free, green, lambda c: move(CROSS, green, (partner, 2), c).start())
         for c in range(CHUNKS):
             move(NEAR, green, (partner, s), c).start()
+        load_screened()
         sum_weights()
+        meet_onward()
         for c in range(CHUNKS):
             arrived(NEAR, c)
             move(CHAIN, near, (partner, 2), c).start()
@@ -228,43 +266,46 @@
     @pl.when(s == 2)
     def _():
         load_free.wait()
-        pl.semaphore_wait(barrier, 3)
+        meet(2, 0)
         for c in range(CHUNKS):
             move(FREE_NEAR, free, (partner, s), c).start()
         load_coup.wait()
+        load_screened()
         maps(free, OWN)
         sum_weights()
         all_arrived(FREE_NEAR)
         maps(free_near, BESIDE)
+        meet_onward()
         all_arrived(CROSS)
 
         def hand_on(c):
-            move(FAR, near, (onward, s), c).start()
+            move(BEYOND, near, (onward, 3), c).start()
             move(CROSS, near, (e, 3), c).start()
 
         advance(BESIDE, cross_in, free_near, near, hand_on)
         all_arrived(CHAIN)
         advance(OWN, chain_in, free, green, lambda c: move(CHAIN, green, (e, 3), c).start())
         for c in range(CHUNKS):
+            begin_sigma(c)
+        for c in range(CHUNKS):
             arrived(FAR, c)
-            move(BEYOND, far, (e, 3), c).start()
-            begin_sigma(c)
             end_sigma(c)
         sent(FREE_NEAR)
-        sent(FAR)
+        sent(BEYOND)
         sent(CROSS)
         sent(CHAIN)
-        sent(BEYOND)
 
     @pl.when(s == 3)
     def _():
         load_free.wait()
         load_coup.wait()
+        load_screened()
         maps(free, OWN)
         sum_weights()
-        pl.semaphore_wait(barrier, 2)
+        meet(2, 2)
         for c in range(CHUNKS):
             move(FREE_NEAR, free, (partner, s), c).start()
+        meet_onward()
         for c in range(CHUNKS):
             arrived(FREE_NEAR, c)
             move(FREE_FAR, free_near, (onward, s), c).start()
@@ -277,10 +318,13 @@
         advance(OWN, chain_in, free, green)
         for c in range(CHUNKS):
             begin_sigma(c)
-        all_arrived(BEYOND)
+        for c in range(CHUNKS):
+            arrived(BEYOND, c)
+            move(FAR, beyond_in, (e, 2), c).start()
         advance(REMOTE, beyond_in, free_far, far, end_sigma)
         sent(FREE_NEAR)
         sent(FREE_FAR)
+        sent(FAR)
 
 
 def store(green, sig, green_hbm, sigma_hbm, sem):
@@ -319,6 +363,7 @@
             dma((2 + shifts,)),
             dma((7, CHUNKS)),
             dma((7, CHUNKS)),
+            pltpu.SemaphoreType.REGULAR,
         ],
         compiler_params=pltpu.CompilerParams(
             collective_id=0, has_side_effects=True, vmem_limit_bytes=57 * 2**20

time: 39 us -> 37.7 us (0.967)
  Pallas kernels: 38.1 us -> 36.8 us
    pallas_call x1, Pallas kernels: 37.2 us -> 35.9 us  [shards(): pl.pallas_call(functools.partial(kernel, energies), out_shape=(pltpu.VMEM...]
where the time goes in v3:
time: 37.7 us; the launch traced here: 37.5 us
  Pallas kernels  36.8 us (98%)
  between operations  0.64 us (2%)
    pallas_call x1, Pallas kernels, shards(): pl.pallas_call(functools.partial(kernel, energies), out_shape=(pltpu.VMEM...  35.9 us
    pallas_call x1, Pallas kernels, shards(): pl.pallas_call(store, out_shape=(jax.ShapeDtypeStruct(green_free.shape, h...  0.9 us

profile of v3, /device:TPU:5, one launch (start us, length us, event | category | flops | bytes accessed | tf_op | source)
XLA Modules:
  0.0 37.5 jit_solution(13760384303687815837)
XLA Ops:
  0.6 35.9 %shard_map.59 = (bf16[2,256,256]{2,1,0:T(8,128)(2,1)S(1)}, f32[2,256,256]{2,1,0:T(8,128)S(1)}) custom-call(s32[8]{0:T(128)} %shift_ref.1, bf16[1,1,2,256,256]{4,3,2,1,0:T(8,128)(2,1)} %free_hbm.1, bf16[1,2,256,256]{3,2,1,0:T(8,128)(2,1)} %coup_hbm.1, bf16[8,1,2,256,256]{4,3,2,1,0:T(8,128)(2,1)} %scr_hbm.1), custom_call_target="tpu_custom_call" | custom-call | tf_op jit(solution)/shard_map/pallas_call | solution.py:350
  36.6 0.9 %shard_map.60 = (bf16[1,1,2,256,256]{4,3,2,1,0:T(8,128)(2,1)}, f32[1,1,2,256,256]{4,3,2,1,0:T(8,128)}) custom-call(bf16[2,256,256]{2,1,0:T(8,128)(2,1)S(1)} %get-tuple-element.4.green, f32[2,256,256]{2,1,0:T(8,128)S(1)} %get-tuple-element.5.sig), custom_call_target="tpu_custom_call" | custom-call | tf_op jit(solution)/shard_map/pallas_call | solution.py:372

commit v4 on v3

--- a/solution.py
+++ b/solution.py
@@ -10,7 +10,7 @@
 MESH = pl.DeviceIdType.MESH
 CHUNKS = 4
 STEPS = 2
-CHAIN, CROSS, BEYOND, NEAR, FAR, FREE_NEAR, FREE_FAR = range(7)
+CHAIN, CROSS, BEYOND, NEAR, FAR, FREE_NEAR, FREE_FAR, WRAP, WRAP_TWO = range(9)
 OWN, BESIDE, REMOTE = range(3)
 
 
@@ -55,6 +55,7 @@
     send_sem,
     recv_sem,
     ready,
+    near_ready,
 ):
     e = lax.axis_index("energy")
     s = lax.axis_index("slab")
@@ -78,7 +79,15 @@
     def greet(device):
         pl.semaphore_signal(barrier, inc=1, device_id=device, device_id_type=MESH)
 
-    greet((partner, s))
+    last = energies - 1
+    is_first = e == 0
+    is_last = e == last
+    has_onward = e != last - 1
+    far_side = jnp.where(s == 2, 3, s)
+
+    @pl.when(jnp.logical_or(e > 0, s > 0))
+    def _():
+        greet((partner, s))
 
     @pl.when(s == 1)
     def _():
@@ -93,25 +102,32 @@
     def _():
         greet((e, 2))
 
-    far_side = jnp.where(s == 2, 3, s)
-
     @pl.when(onward > e)
     def _():
         greet((onward, far_side))
 
-    @pl.when(jnp.logical_and(behind > e, s != 2))
+    @pl.when(jnp.logical_and(e > 0, jnp.logical_and(behind > e, s != 2)))
     def _():
         greet((behind, s))
 
-    @pl.when(jnp.logical_and(behind > e, s == 3))
+    @pl.when(jnp.logical_and(e > 0, jnp.logical_and(behind > e, s == 3)))
     def _():
         greet((behind, 2))
+
+    @pl.when(is_first)
+    def _():
+        greet((last, s))
+
+    @pl.when(jnp.logical_and(is_first, s == 2))
+    def _():
+        greet((last, 1))
 
     load_free.start()
     load_coup.start()
 
-    def meet(row, senders):
-        below = jnp.where(onward < e, 1, 0) + jnp.where(behind < e, senders, 0)
+    def meet(row, senders, wrapped):
+        below = jnp.where(jnp.logical_and(has_onward, onward < e), 1, 0)
+        below = below + jnp.where(behind < e, senders, 0) + jnp.where(is_last, wrapped, 0)
         pl.semaphore_wait(barrier, row + below)
         if senders:
 
@@ -131,12 +147,13 @@
         for load in loads:
             load.start()
 
-    def move(kind, source, device, c):
+    def move(kind, source, device, c, sender=None):
+        sender = kind if sender is None else sender
         part = pl.ds(c * rows, rows)
         return pltpu.make_async_remote_copy(
             src_ref=source.at[:, part],
             dst_ref=landing[kind].at[:, part],
-            send_sem=send_sem.at[kind, c],
+            send_sem=send_sem.at[sender, c],
             recv_sem=recv_sem.at[kind, c],
             device_id=device,
             device_id_type=MESH,
@@ -151,7 +168,7 @@
 
     def sent(kind):
         for c in range(CHUNKS):
-            move(kind, free, (partner, s), c).wait_send()
+            move(0, free, (partner, s), c, kind).wait_send()
 
     def maps(block, slot):
         re, im = complex_dot(block[...].reshape(2 * orb, orb), coup[0], coup[1])
@@ -216,9 +233,24 @@
     @pl.when(s == 0)
     def _():
         load_free.wait()
-        meet(2, 1)
+        meet(jnp.where(e == 1, 1, 2), 1, 1)
         for c in range(CHUNKS):
             move(CHAIN, free, (e, 1), c).start()
+
+        @pl.when(is_last)
+        def _():
+            for c in range(CHUNKS):
+                move(FAR, free, (0, s), c, WRAP).start()
+            sent(WRAP)
+
+        @pl.when(is_first)
+        def _():
+            pl.semaphore_signal(near_ready, inc=1, device_id=(1, 0), device_id_type=MESH)
+
+        @pl.when(e == 1)
+        def _():
+            pl.semaphore_wait(near_ready, 1)
+
         for c in range(CHUNKS):
             move(NEAR, free, (partner, s), c).start()
         load_screened()
@@ -227,7 +259,11 @@
         meet_onward()
         for c in range(CHUNKS):
             arrived(NEAR, c)
-            move(FAR, near, (onward, s), c).start()
+
+            @pl.when(has_onward)
+            def _():
+                move(FAR, near, (onward, s), c).start()
+
             begin_sigma(c)
         for c in range(CHUNKS):
             arrived(FAR, c)
@@ -235,25 +271,66 @@
         load_coup.wait()
         sent(CHAIN)
         sent(NEAR)
-        sent(FAR)
+
+        @pl.when(has_onward)
+        def _():
+            sent(FAR)
 
     @pl.when(s == 1)
     def _():
+        def relay(c):
+            arrived(NEAR, c)
+            move(CHAIN, near, (partner, 2), c).start()
+
         load_free.wait()
         load_coup.wait()
         maps(free, OWN)
-        meet(2, 1)
+        meet(2, 1, 2)
+
+        @pl.when(is_first)
+        def _():
+            for c in range(CHUNKS):
+                relay(c)
+
         all_arrived(CHAIN)
-        advance(OWN, chain_in, free, green, lambda c: move(CROSS, green, (partner, 2), c).start())
+
+        def hand_on(c):
+            @pl.when(is_last)
+            def _():
+                move(BEYOND, green, (0, 2), c, WRAP).start()
+
+            @pl.when(jnp.logical_not(is_last))
+            def _():
+                move(CROSS, green, (partner, 2), c).start()
+
+        advance(OWN, chain_in, free, green, hand_on)
+
+        @pl.when(is_last)
+        def _():
+            for c in range(CHUNKS):
+                move(FAR, green, (0, 1), c, WRAP_TWO).start()
+            sent(WRAP)
+            for c in range(CHUNKS):
+                move(CROSS, green, (partner, 2), c).start()
+            sent(WRAP_TWO)
+
         for c in range(CHUNKS):
             move(NEAR, green, (partner, s), c).start()
         load_screened()
         sum_weights()
+
+        @pl.when(e > 0)
+        def _():
+            for c in range(CHUNKS):
+                relay(c)
+
         meet_onward()
         for c in range(CHUNKS):
-            arrived(NEAR, c)
-            move(CHAIN, near, (partner, 2), c).start()
-            move(FAR, near, (onward, s), c).start()
+
+            @pl.when(has_onward)
+            def _():
+                move(FAR, near, (onward, s), c).start()
+
             begin_sigma(c)
         for c in range(CHUNKS):
             arrived(FAR, c)
@@ -261,12 +338,21 @@
         sent(CROSS)
         sent(NEAR)
         sent(CHAIN)
-        sent(FAR)
+
+        @pl.when(has_onward)
+        def _():
+            sent(FAR)
 
     @pl.when(s == 2)
     def _():
         load_free.wait()
-        meet(2, 0)
+        meet(2, 0, 1)
+
+        @pl.when(is_last)
+        def _():
+            for c in range(CHUNKS):
+                move(FREE_FAR, free, (0, 2), c, WRAP).start()
+
         for c in range(CHUNKS):
             move(FREE_NEAR, free, (partner, s), c).start()
         load_coup.wait()
@@ -275,25 +361,50 @@
         sum_weights()
         all_arrived(FREE_NEAR)
         maps(free_near, BESIDE)
+        all_arrived(CROSS)
+        advance(BESIDE, cross_in, free_near, near, lambda c: move(CROSS, near, (e, 3), c).start())
         meet_onward()
-        all_arrived(CROSS)
-
-        def hand_on(c):
-            move(BEYOND, near, (onward, 3), c).start()
-            move(CROSS, near, (e, 3), c).start()
-
-        advance(BESIDE, cross_in, free_near, near, hand_on)
+
+        @pl.when(has_onward)
+        def _():
+            for c in range(CHUNKS):
+                move(BEYOND, near, (onward, 3), c).start()
+
         all_arrived(CHAIN)
         advance(OWN, chain_in, free, green, lambda c: move(CHAIN, green, (e, 3), c).start())
         for c in range(CHUNKS):
             begin_sigma(c)
-        for c in range(CHUNKS):
-            arrived(FAR, c)
+
+        @pl.when(is_first)
+        def _():
+            all_arrived(FREE_FAR)
+            maps(free_far, REMOTE)
+            all_arrived(BEYOND)
+            advance(
+                REMOTE,
+                beyond_in,
+                free_far,
+                far,
+                lambda c: move(BEYOND, far, (e, 3), c, WRAP).start(),
+            )
+
+        @pl.when(e > 0)
+        def _():
+            all_arrived(FAR)
+
+        for c in range(CHUNKS):
             end_sigma(c)
         sent(FREE_NEAR)
-        sent(BEYOND)
         sent(CROSS)
         sent(CHAIN)
+
+        @pl.when(has_onward)
+        def _():
+            sent(BEYOND)
+
+        @pl.when(jnp.logical_or(is_first, is_last))
+        def _():
+            sent(WRAP)
 
     @pl.when(s == 3)
     def _():
@@ -302,29 +413,60 @@
         load_screened()
         maps(free, OWN)
         sum_weights()
-        meet(2, 2)
+        meet(2, 2, 1)
+
+        @pl.when(is_last)
+        def _():
+            for c in range(CHUNKS):
+                move(FREE_FAR, free, (0, 3), c, WRAP).start()
+            sent(WRAP)
+
         for c in range(CHUNKS):
             move(FREE_NEAR, free, (partner, s), c).start()
         meet_onward()
         for c in range(CHUNKS):
             arrived(FREE_NEAR, c)
-            move(FREE_FAR, free_near, (onward, s), c).start()
+
+            @pl.when(has_onward)
+            def _():
+                move(FREE_FAR, free_near, (onward, s), c).start()
+
         maps(free_near, BESIDE)
         all_arrived(CROSS)
         advance(BESIDE, cross_in, free_near, near)
-        all_arrived(FREE_FAR)
-        maps(free_far, REMOTE)
+
+        @pl.when(e > 0)
+        def _():
+            all_arrived(FREE_FAR)
+            maps(free_far, REMOTE)
+
         all_arrived(CHAIN)
         advance(OWN, chain_in, free, green)
         for c in range(CHUNKS):
             begin_sigma(c)
+
+        @pl.when(is_first)
+        def _():
+            all_arrived(FREE_FAR)
+            maps(free_far, REMOTE)
+
         for c in range(CHUNKS):
             arrived(BEYOND, c)
-            move(FAR, beyond_in, (e, 2), c).start()
+
+            @pl.when(e > 0)
+            def _():
+                move(FAR, beyond_in, (e, 2), c).start()
+
         advance(REMOTE, beyond_in, free_far, far, end_sigma)
         sent(FREE_NEAR)
-        sent(FREE_FAR)
-        sent(FAR)
+
+        @pl.when(has_onward)
+        def _():
+            sent(FREE_FAR)
+
+        @pl.when(e > 0)
+        def _():
+            sent(FAR)
 
 
 def store(green, sig, green_hbm, sigma_hbm, sem):
@@ -361,8 +503,9 @@
             *[pltpu.VMEM(block, half)] * 8,
             pltpu.VMEM((3, *block), jnp.float32),
             dma((2 + shifts,)),
+            dma((9, CHUNKS)),
             dma((7, CHUNKS)),
-            dma((7, CHUNKS)),
+            pltpu.SemaphoreType.REGULAR,
             pltpu.SemaphoreType.REGULAR,
         ],
         compiler_params=pltpu.CompilerParams(

time: 37.7 us -> 36.9 us (0.979)
  Pallas kernels: 36.8 us -> 36.1 us
    pallas_call x1, Pallas kernels: 35.9 us -> 35.2 us  [shards(): pl.pallas_call(functools.partial(kernel, energies), out_shape=(pltpu.VMEM...]
where the time goes in v4:
time: 36.9 us; the launch traced here: 36.7 us
  Pallas kernels  36.1 us (98%)
  between operations  0.64 us (2%)
    pallas_call x1, Pallas kernels, shards(): pl.pallas_call(functools.partial(kernel, energies), out_shape=(pltpu.VMEM...  35.2 us
    pallas_call x1, Pallas kernels, shards(): pl.pallas_call(store, out_shape=(jax.ShapeDtypeStruct(green_free.shape, h...  0.9 us

profile of v4, /device:TPU:5, one launch (start us, length us, event | category | flops | bytes accessed | tf_op | source)
XLA Modules:
  0.0 36.7 jit_solution(4527434948177210558)
XLA Ops:
  0.6 35.2 %shard_map.59 = (bf16[2,256,256]{2,1,0:T(8,128)(2,1)S(1)}, f32[2,256,256]{2,1,0:T(8,128)S(1)}) custom-call(s32[8]{0:T(128)} %shift_ref.1, bf16[1,1,2,256,256]{4,3,2,1,0:T(8,128)(2,1)} %free_hbm.1, bf16[1,2,256,256]{3,2,1,0:T(8,128)(2,1)} %coup_hbm.1, bf16[8,1,2,256,256]{4,3,2,1,0:T(8,128)(2,1)} %scr_hbm.1), custom_call_target="tpu_custom_call" | custom-call | tf_op jit(solution)/shard_map/pallas_call | solution.py:492
  35.8 0.9 %shard_map.60 = (bf16[1,1,2,256,256]{4,3,2,1,0:T(8,128)(2,1)}, f32[1,1,2,256,256]{4,3,2,1,0:T(8,128)}) custom-call(bf16[2,256,256]{2,1,0:T(8,128)(2,1)S(1)} %get-tuple-element.4.green, f32[2,256,256]{2,1,0:T(8,128)S(1)} %get-tuple-element.5.sig), custom_call_target="tpu_custom_call" | custom-call | tf_op jit(solution)/shard_map/pallas_call | solution.py:515

commit v5 on v4

--- a/solution.py
+++ b/solution.py
@@ -10,7 +10,7 @@
 MESH = pl.DeviceIdType.MESH
 CHUNKS = 4
 STEPS = 2
-CHAIN, CROSS, BEYOND, NEAR, FAR, FREE_NEAR, FREE_FAR, WRAP, WRAP_TWO = range(9)
+CHAIN, CROSS, BEYOND, NEAR, FAR, FREE_NEAR, FREE_FAR, SEAM, WRAP, WRAP_TWO = range(10)
 OWN, BESIDE, REMOTE = range(3)
 
 
@@ -50,6 +50,7 @@
     far,
     free_near,
     free_far,
+    seam_in,
     weight,
     load_sem,
     send_sem,
@@ -66,7 +67,7 @@
     partner = e + 1 - 2 * parity
     onward = lax.rem(e + 2 - 4 * parity + energies, energies)
     behind = lax.rem(e - 2 + 4 * parity + energies, energies)
-    landing = (chain_in, cross_in, beyond_in, near, far, free_near, free_far)
+    landing = (chain_in, cross_in, beyond_in, near, far, free_near, free_far, seam_in)
 
     load_free = pltpu.make_async_copy(free_hbm.at[0, 0], free, load_sem.at[0])
     load_coup = pltpu.make_async_copy(coup_hbm.at[0], coup, load_sem.at[1])
@@ -85,7 +86,9 @@
     has_onward = e != last - 1
     far_side = jnp.where(s == 2, 3, s)
 
-    @pl.when(jnp.logical_or(e > 0, s > 0))
+    lead = jnp.logical_and(is_last, s == 0)
+
+    @pl.when(jnp.logical_or(s > 0, jnp.logical_and(e > 0, has_onward)))
     def _():
         greet((partner, s))
 
@@ -102,11 +105,14 @@
     def _():
         greet((e, 2))
 
-    @pl.when(onward > e)
+    @pl.when(jnp.logical_or(onward > e, lead))
     def _():
         greet((onward, far_side))
 
-    @pl.when(jnp.logical_and(e > 0, jnp.logical_and(behind > e, s != 2)))
+    led = jnp.logical_and(e == last - 2, s == 0)
+    greets_behind = jnp.logical_and(behind > e, jnp.logical_not(led))
+
+    @pl.when(jnp.logical_and(e > 0, jnp.logical_and(greets_behind, s != 2)))
     def _():
         greet((behind, s))
 
@@ -114,9 +120,13 @@
     def _():
         greet((behind, 2))
 
-    @pl.when(is_first)
-    def _():
-        greet((last, s))
+    @pl.when(jnp.logical_and(is_first, s < 3))
+    def _():
+        greet((last, jnp.where(s == 2, 2, 0)))
+
+    @pl.when(jnp.logical_and(is_last, s == 0))
+    def _():
+        greet((last, 1))
 
     @pl.when(jnp.logical_and(is_first, s == 2))
     def _():
@@ -126,12 +136,14 @@
     load_coup.start()
 
     def meet(row, senders, wrapped):
-        below = jnp.where(jnp.logical_and(has_onward, onward < e), 1, 0)
-        below = below + jnp.where(behind < e, senders, 0) + jnp.where(is_last, wrapped, 0)
+        waits = jnp.logical_and(has_onward, jnp.logical_and(onward < e, jnp.logical_not(lead)))
+        answers = jnp.logical_or(behind < e, led)
+        below = jnp.where(waits, 1, 0) + jnp.where(is_last, wrapped, 0)
+        below = below + jnp.where(answers, senders, 0)
         pl.semaphore_wait(barrier, row + below)
         if senders:
 
-            @pl.when(behind < e)
+            @pl.when(answers)
             def _():
                 for sender in range(senders):
                     pl.semaphore_signal(
@@ -139,7 +151,7 @@
                     )
 
     def meet_onward():
-        @pl.when(onward > e)
+        @pl.when(jnp.logical_or(onward > e, lead))
         def _():
             pl.semaphore_wait(ready, 1)
 
@@ -232,27 +244,32 @@
 
     @pl.when(s == 0)
     def _():
+        meet(jnp.where(jnp.logical_or(e == 1, is_last), 1, 2), 1, 2)
+        for c in range(CHUNKS):
+            move(CHAIN, free_hbm.at[0, 0], (e, 1), c).start()
         load_free.wait()
-        meet(jnp.where(e == 1, 1, 2), 1, 1)
-        for c in range(CHUNKS):
-            move(CHAIN, free, (e, 1), c).start()
 
         @pl.when(is_last)
         def _():
             for c in range(CHUNKS):
                 move(FAR, free, (0, s), c, WRAP).start()
-            sent(WRAP)
-
-        @pl.when(is_first)
-        def _():
-            pl.semaphore_signal(near_ready, inc=1, device_id=(1, 0), device_id_type=MESH)
+            for c in range(CHUNKS):
+                arrived(SEAM, c)
+                move(FAR, seam_in, (0, 1), c, WRAP_TWO).start()
+
+        @pl.when(jnp.logical_or(is_first, e == last - 1))
+        def _():
+            pl.semaphore_signal(near_ready, inc=1, device_id=(partner, 0), device_id_type=MESH)
 
         @pl.when(e == 1)
         def _():
             pl.semaphore_wait(near_ready, 1)
 
-        for c in range(CHUNKS):
-            move(NEAR, free, (partner, s), c).start()
+        @pl.when(jnp.logical_not(is_last))
+        def _():
+            for c in range(CHUNKS):
+                move(NEAR, free, (partner, s), c).start()
+
         load_screened()
         green[...] = free[...]
         sum_weights()
@@ -265,6 +282,13 @@
                 move(FAR, near, (onward, s), c).start()
 
             begin_sigma(c)
+
+        @pl.when(is_last)
+        def _():
+            pl.semaphore_wait(near_ready, 1)
+            for c in range(CHUNKS):
+                move(NEAR, free, (partner, s), c).start()
+
         for c in range(CHUNKS):
             arrived(FAR, c)
             end_sigma(c)
@@ -272,6 +296,11 @@
         sent(CHAIN)
         sent(NEAR)
 
+        @pl.when(is_last)
+        def _():
+            sent(WRAP)
+            sent(WRAP_TWO)
+
         @pl.when(has_onward)
         def _():
             sent(FAR)
@@ -308,11 +337,11 @@
         @pl.when(is_last)
         def _():
             for c in range(CHUNKS):
-                move(FAR, green, (0, 1), c, WRAP_TWO).start()
+                move(SEAM, green, (e, 0), c).start()
             sent(WRAP)
             for c in range(CHUNKS):
                 move(CROSS, green, (partner, 2), c).start()
-            sent(WRAP_TWO)
+            sent(SEAM)
 
         for c in range(CHUNKS):
             move(NEAR, green, (partner, s), c).start()
@@ -352,6 +381,7 @@
         def _():
             for c in range(CHUNKS):
                 move(FREE_FAR, free, (0, 2), c, WRAP).start()
+            sent(WRAP)
 
         for c in range(CHUNKS):
             move(FREE_NEAR, free, (partner, s), c).start()
@@ -402,7 +432,7 @@
         def _():
             sent(BEYOND)
 
-        @pl.when(jnp.logical_or(is_first, is_last))
+        @pl.when(is_first)
         def _():
             sent(WRAP)
 
@@ -411,15 +441,19 @@
         load_free.wait()
         load_coup.wait()
         load_screened()
+        meet(2, 2, 0)
+
+        @pl.when(is_last)
+        def _():
+            for c in range(CHUNKS):
+                move(SEAM, free, (1, 3), c).start()
+
         maps(free, OWN)
         sum_weights()
-        meet(2, 2, 1)
-
-        @pl.when(is_last)
-        def _():
-            for c in range(CHUNKS):
-                move(FREE_FAR, free, (0, 3), c, WRAP).start()
-            sent(WRAP)
+
+        @pl.when(is_last)
+        def _():
+            sent(SEAM)
 
         for c in range(CHUNKS):
             move(FREE_NEAR, free, (partner, s), c).start()
@@ -442,6 +476,13 @@
 
         all_arrived(CHAIN)
         advance(OWN, chain_in, free, green)
+
+        @pl.when(e == 1)
+        def _():
+            for c in range(CHUNKS):
+                arrived(SEAM, c)
+                move(FREE_FAR, seam_in, (0, 3), c, WRAP).start()
+
         for c in range(CHUNKS):
             begin_sigma(c)
 
@@ -459,6 +500,10 @@
 
         advance(REMOTE, beyond_in, free_far, far, end_sigma)
         sent(FREE_NEAR)
+
+        @pl.when(e == 1)
+        def _():
+            sent(WRAP)
 
         @pl.when(has_onward)
         def _():
@@ -500,11 +545,11 @@
             pltpu.VMEM((shifts, *block), half),
             pltpu.VMEM((3, *block), half),
             pltpu.VMEM((3, *block), half),
-            *[pltpu.VMEM(block, half)] * 8,
+            *[pltpu.VMEM(block, half)] * 9,
             pltpu.VMEM((3, *block), jnp.float32),
             dma((2 + shifts,)),
-            dma((9, CHUNKS)),
-            dma((7, CHUNKS)),
+            dma((10, CHUNKS)),
+            dma((8, CHUNKS)),
             pltpu.SemaphoreType.REGULAR,
             pltpu.SemaphoreType.REGULAR,
         ],

time: 36.9 us -> 35.9 us (0.973)
  the two profiles are of different devices: /device:TPU:5 before, /device:TPU:1 now
where the time goes in v5:
time: 35.9 us; the launch traced here: 35.7 us
  Pallas kernels  35.1 us (98%)
  between operations  0.64 us (2%)
    pallas_call x1, Pallas kernels, shards(): pl.pallas_call(functools.partial(kernel, energies), out_shape=(pltpu.VMEM...  34.2 us
    pallas_call x1, Pallas kernels, shards(): pl.pallas_call(store, out_shape=(jax.ShapeDtypeStruct(green_free.shape, h...  0.9 us

profile of v5, /device:TPU:1, one launch (start us, length us, event | category | flops | bytes accessed | tf_op | source)
XLA Modules:
  0.0 35.7 jit_solution(15310896520101223838)
XLA Ops:
  0.6 34.2 %shard_map.59 = (bf16[2,256,256]{2,1,0:T(8,128)(2,1)S(1)}, f32[2,256,256]{2,1,0:T(8,128)S(1)}) custom-call(s32[8]{0:T(128)} %shift_ref.1, bf16[1,1,2,256,256]{4,3,2,1,0:T(8,128)(2,1)} %free_hbm.1, bf16[1,2,256,256]{3,2,1,0:T(8,128)(2,1)} %coup_hbm.1, bf16[8,1,2,256,256]{4,3,2,1,0:T(8,128)(2,1)} %scr_hbm.1), custom_call_target="tpu_custom_call" | custom-call | tf_op jit(solution)/shard_map/pallas_call | solution.py:537
  34.8 0.9 %shard_map.60 = (bf16[1,1,2,256,256]{4,3,2,1,0:T(8,128)(2,1)}, f32[1,1,2,256,256]{4,3,2,1,0:T(8,128)}) custom-call(bf16[2,256,256]{2,1,0:T(8,128)(2,1)S(1)} %get-tuple-element.4.green, f32[2,256,256]{2,1,0:T(8,128)S(1)} %get-tuple-element.5.sig), custom_call_target="tpu_custom_call" | custom-call | tf_op jit(solution)/shard_map/pallas_call | solution.py:560

commit v6 on v5

--- a/solution.py
+++ b/solution.py
@@ -8,7 +8,7 @@
 from jax.sharding import PartitionSpec as P
 
 MESH = pl.DeviceIdType.MESH
-CHUNKS = 4
+CHUNKS = 2
 STEPS = 2
 CHAIN, CROSS, BEYOND, NEAR, FAR, FREE_NEAR, FREE_FAR, SEAM, WRAP, WRAP_TWO = range(10)
 OWN, BESIDE, REMOTE = range(3)

time: 35.9 us -> 35.6 us (level)
  no operation moved by 1% of the time
where the time goes in v6:
time: 35.6 us; the launch traced here: 35.4 us
  Pallas kernels  34.8 us (98%)
  between operations  0.64 us (2%)
    pallas_call x1, Pallas kernels, shards(): pl.pallas_call(functools.partial(kernel, energies), out_shape=(pltpu.VMEM...  33.8 us
    pallas_call x1, Pallas kernels, shards(): pl.pallas_call(store, out_shape=(jax.ShapeDtypeStruct(green_free.shape, h...  0.9 us

profile of v6, /device:TPU:1, one launch (start us, length us, event | category | flops | bytes accessed | tf_op | source)
XLA Modules:
  0.0 35.4 jit_solution(3183331429034860770)
XLA Ops:
  0.6 33.8 %shard_map.59 = (bf16[2,256,256]{2,1,0:T(8,128)(2,1)S(1)}, f32[2,256,256]{2,1,0:T(8,128)S(1)}) custom-call(s32[8]{0:T(128)} %shift_ref.1, bf16[1,1,2,256,256]{4,3,2,1,0:T(8,128)(2,1)} %free_hbm.1, bf16[1,2,256,256]{3,2,1,0:T(8,128)(2,1)} %coup_hbm.1, bf16[8,1,2,256,256]{4,3,2,1,0:T(8,128)(2,1)} %scr_hbm.1), custom_call_target="tpu_custom_call" | custom-call | tf_op jit(solution)/shard_map/pallas_call | solution.py:537
  34.5 0.9 %shard_map.60 = (bf16[1,1,2,256,256]{4,3,2,1,0:T(8,128)(2,1)}, f32[1,1,2,256,256]{4,3,2,1,0:T(8,128)}) custom-call(bf16[2,256,256]{2,1,0:T(8,128)(2,1)S(1)} %get-tuple-element.4.green, f32[2,256,256]{2,1,0:T(8,128)S(1)} %get-tuple-element.5.sig), custom_call_target="tpu_custom_call" | custom-call | tf_op jit(solution)/shard_map/pallas_call | solution.py:560
